TPU v7x, 32 devices: a whole 2x2x4 slice. The times are simulated.
32 devices in a mesh: ctx: 8 (over y, x, core), kv: 4 (over z).
Axes of the slice: x: 2, y: 2, z: 4, core: 2. Of those that a mesh axis runs over, the one named last changes fastest.
Arguments:
- queries: bfloat16 [3072, 64, 128], P('ctx', 'kv'), may hold values from -128 to 128
- key_heads: bfloat16 [3072, 8, 128], P('ctx', 'kv'), may hold values from -6 to 6
- value_heads: bfloat16 [3072, 8, 128], P('ctx', 'kv'), may hold values from -6 to 6
- grad_out: bfloat16 [3072, 64, 128], P('ctx', 'kv'), may hold values from -6 to 6
- transforms: float32 [8, 128, 128], P('ctx'), may hold values from -1.2 to 1.2
- window: int32 [8], P('kv'), may hold values from 1 to 4, as said below
- first_block: int32 [1], replicated, may hold values from 0 to 7
Outputs:
- query_grad: bfloat16 [3072, 64, 128], P('ctx', 'kv')
- key_grad: bfloat16 [3072, 8, 128], P('ctx', 'kv')
- value_grad: bfloat16 [3072, 8, 128], P('ctx', 'kv')
- turn_grad: float32 [8, 128, 128], P('ctx')
Inputs may be any that keep to these rules, and one draw needn't show every extreme that they name: Some key-value head has a window of 4 blocks.
All inputs are finite; a program needn't handle non-finite values.
Results may differ from a plain program's by a relative error of at most 0.019.
Values may be sent and summed in bfloat16 or wider, within the bound.
A program may use at most 256 MiB of HBM per device.

v0:
```python
import math

import jax
import jax.numpy as jnp
from jax import lax
from jax.experimental import pallas as pl
from jax.experimental.pallas import tpu as pltpu
from jax.sharding import PartitionSpec as P

HOPS = 3
CHUNK = 128
HALF = jnp.bfloat16
FULL = jnp.float32
PRECISE = lax.Precision.HIGHEST
NT = (((1,), (1,)), ((), ()))
TN = (((0,), (0,)), ((), ()))


def passed_along(shard, by):
    peers = lax.axis_size("ctx")
    return lax.ppermute(shard, "ctx", [(i, (i + by) % peers) for i in range(peers)])


def split_parts(matrix):
    upper = matrix.astype(HALF)
    lower = (matrix - upper.astype(FULL)).astype(HALF)
    return (upper, lower)


def times_split(rows_half, matrix, spec):
    upper, lower = split_parts(matrix)
    first = jnp.einsum(spec, rows_half, upper, preferred_element_type=FULL)
    return first + jnp.einsum(spec, rows_half, lower, preferred_element_type=FULL)


def attention_kernel(groups, factor, hops_ref, q_ref, g_ref, *refs):
    kv_refs = refs[: HOPS + 1]
    dq_ref, dk_ref, dv_ref, e_ref, slope_ref, max_ref, dk_acc, dv_acc, dq_acc = refs[HOPS + 1 :]
    tile = pl.program_id(0)
    tiles = pl.num_programs(0)
    rows = q_ref.shape[0]
    per_hop = kv_refs[0].shape[1] // CHUNK
    scale = factor * math.log2(math.e)
    hop_count = hops_ref[0]

    @pl.when(tile == 0)
    def _():
        dk_acc[...] = jnp.zeros_like(dk_acc)
        dv_acc[...] = jnp.zeros_like(dv_acc)

    def forward(keys, values, slot, state, masked):
        top, total, dot = state
        logits = lax.dot_general(keys, q_ref[...], NT, preferred_element_type=FULL) * scale
        if masked:
            key_at = lax.broadcasted_iota(jnp.int32, (CHUNK, rows), 0)
            row_at = lax.broadcasted_iota(jnp.int32, (CHUNK, rows), 1) // groups
            logits = jnp.where(key_at <= row_at, logits, -jnp.inf)
        slopes = lax.dot_general(values, g_ref[...], NT, preferred_element_type=FULL)
        chunk_max = jnp.max(logits, axis=0, keepdims=True)
        exps = jnp.exp2(logits - chunk_max)
        e_ref[slot] = exps
        slope_ref[slot] = slopes
        max_ref[slot] = chunk_max
        top_new = jnp.maximum(top, chunk_max)
        old, new = jnp.exp2(top - top_new), jnp.exp2(chunk_max - top_new)
        total = total * old + jnp.sum(exps, axis=0, keepdims=True) * new
        dot = dot * old + jnp.sum(exps * slopes, axis=0, keepdims=True) * new
        return top_new, total, dot

    def backward(keys, slot, state):
        top, inverse, dot = state
        part = jnp.exp2(max_ref[slot] - top) * inverse
        weights = e_ref[slot] * part
        scores = (weights * (slope_ref[slot] - dot)).astype(HALF)
        spot = pl.ds(pl.multiple_of(slot * CHUNK, CHUNK), CHUNK)
        dv_acc[spot, :] += jnp.dot(weights.astype(HALF), g_ref[...], preferred_element_type=FULL)
        dk_acc[spot, :] += jnp.dot(scores, q_ref[...], preferred_element_type=FULL)
        dq_acc[...] += lax.dot_general(keys, scores, TN, preferred_element_type=FULL)

    def spot_of(index):
        return pl.ds(pl.multiple_of(index * CHUNK, CHUNK), CHUNK)

    state = (
        jnp.full((1, rows), -jnp.inf, FULL),
        jnp.zeros((1, rows), FULL),
        jnp.zeros((1, rows), FULL),
    )
    own = kv_refs[0]
    state = forward(own[0, spot_of(tile), :], own[1, spot_of(tile), :], tile, state, True)
    state = lax.fori_loop(
        0,
        tile,
        lambda i, s: forward(own[0, spot_of(i), :], own[1, spot_of(i), :], i, s, False),
        state,
    )
    for hop in range(1, HOPS + 1):
        ref = kv_refs[hop]
        state = lax.fori_loop(
            0,
            jnp.where(hop < hop_count, per_hop, 0),
            lambda i, s, ref=ref, hop=hop: forward(
                ref[0, spot_of(i), :], ref[1, spot_of(i), :], hop * per_hop + i, s, False
            ),
            state,
        )
    top, total, dot = state
    inverse = 1.0 / total
    final = (top, inverse, dot * inverse)
    dq_acc[...] = jnp.zeros_like(dq_acc)
    for hop in range(HOPS + 1):
        ref = kv_refs[hop]
        trips = tile + 1 if hop == 0 else jnp.where(hop < hop_count, per_hop, 0)

        def step(i, carry, ref=ref, hop=hop):
            backward(ref[0, spot_of(i), :], hop * per_hop + i, final)
            return carry

        lax.fori_loop(0, trips, step, 0)
    dq_ref[...] = (dq_acc[...] * factor).T.astype(HALF)

    @pl.when(tile == tiles - 1)
    def _():
        dk_ref[...] = (dk_acc[...] * factor).astype(HALF)
        dv_ref[...] = dv_acc[...].astype(HALF)


def attention(hop_count, query_rows, grad_rows, pairs, groups, factor):
    total_rows, width = query_rows.shape
    length = pairs[0].shape[1]
    tiles = length // CHUNK
    rows = total_rows // tiles
    hops = len(pairs)
    keys = hops * length
    whole = lambda i: (0, 0, 0)
    row_spec = pl.BlockSpec((rows, width), lambda i: (i, 0))
    part_spec = pl.BlockSpec((keys, width), lambda i: (0, 0))
    chunks = keys // CHUNK
    return pl.pallas_call(
        lambda *refs: attention_kernel(groups, factor, *refs),
        grid=(tiles,),
        in_specs=[pl.BlockSpec(memory_space=pltpu.SMEM), row_spec, row_spec]
        + [pl.BlockSpec((2, length, width), whole)] * hops,
        out_specs=[row_spec, part_spec, part_spec],
        out_shape=[
            jax.ShapeDtypeStruct((total_rows, width), HALF),
            jax.ShapeDtypeStruct((keys, width), HALF),
            jax.ShapeDtypeStruct((keys, width), HALF),
        ],
        scratch_shapes=[
            pltpu.VMEM((chunks, CHUNK, rows), FULL),
            pltpu.VMEM((chunks, CHUNK, rows), FULL),
            pltpu.VMEM((chunks, 1, rows), FULL),
            pltpu.VMEM((keys, width), FULL),
            pltpu.VMEM((keys, width), FULL),
            pltpu.VMEM((width, rows), FULL),
        ],
        compiler_params=pltpu.CompilerParams(vmem_limit_bytes=40 * 1024 * 1024),
        cost_estimate=pl.CostEstimate(
            flops=10 * total_rows * keys * width,
            bytes_accessed=6 * total_rows * width + 8 * keys * width,
            transcendentals=total_rows * keys,
        ),
    )(hop_count, query_rows, grad_rows, *pairs)


def shards(queries, key_heads, value_heads, grad_out, transforms, window, first_block):
    length, head_count, width = queries.shape
    kv_heads = key_heads.shape[1]
    groups = head_count // kv_heads
    factor = 1.0 / math.sqrt(width)
    blocks = lax.axis_size("ctx")
    position = (lax.axis_index("ctx") - first_block[0]) % blocks
    hop_counts = jnp.minimum(window, position + 1)
    turns = [transforms[0]] + [passed_along(transforms[0], -h) for h in range(1, HOPS)]
    chain = [turns[0]]
    for h in range(1, HOPS):
        chain.append(jnp.dot(turns[h], chain[-1], precision=PRECISE))
    own_keys = key_heads.transpose(1, 0, 2)
    own_values = value_heads.transpose(1, 0, 2)
    query_rows = queries.reshape(length, kv_heads, groups, width).transpose(1, 0, 2, 3)
    grad_rows = grad_out.reshape(length, kv_heads, groups, width).transpose(1, 0, 2, 3)
    query_rows = query_rows.reshape(kv_heads, length * groups, width)
    grad_rows = grad_rows.reshape(kv_heads, length * groups, width)
    turned = [own_keys] + [times_split(own_keys, m, "gld,ed->gle").astype(HALF) for m in chain]
    query_parts, key_grads, value_grads = [], [], []
    turn_terms = [jnp.zeros((width, width), FULL) for _ in range(HOPS)]
    for g in range(kv_heads):
        pairs = [jnp.stack([own_keys[g], own_values[g]])]
        for h in range(1, HOPS + 1):
            pairs.append(passed_along(jnp.stack([turned[h][g], own_values[g]]), h))
        dq, dk, dv = attention(
            hop_counts[g : g + 1], query_rows[g], grad_rows[g], pairs, groups, factor
        )
        query_parts.append(dq)
        back = jnp.stack([dk, dv]).reshape(2, HOPS + 1, length, width)
        backs = [back[:, 0]] + [passed_along(back[:, h], -h) for h in range(1, HOPS + 1)]
        carried = backs[HOPS][0].astype(FULL)
        for h in range(HOPS, 0, -1):
            half = carried.astype(HALF)
            turn_terms[h - 1] += lax.dot_general(
                half, turned[h - 1][g], TN, preferred_element_type=FULL
            )
            carried = backs[h - 1][0].astype(FULL) + times_split(half, turns[h - 1], "le,ed->ld")
        key_grads.append(carried.astype(HALF))
        value_grads.append(sum(b[1].astype(FULL) for b in backs).astype(HALF))
    turn_total = turn_terms[0]
    for h in range(1, HOPS):
        turn_total = turn_total + passed_along(turn_terms[h].astype(HALF), h).astype(FULL)
    turn_total = lax.psum(turn_total.astype(HALF), "kv").astype(FULL)
    query_grad = jnp.stack(query_parts).reshape(kv_heads, length, groups, width)
    query_grad = query_grad.transpose(1, 0, 2, 3).reshape(length, head_count, width)
    return (
        query_grad,
        jnp.stack(key_grads, axis=1),
        jnp.stack(value_grads, axis=1),
        turn_total[None],
    )


def solution(mesh):
    return jax.shard_map(
        shards,
        mesh=mesh,
        in_specs=(
            P("ctx", "kv", None),
            P("ctx", "kv", None),
            P("ctx", "kv", None),
            P("ctx", "kv", None),
            P("ctx", None, None),
            P("kv"),
            P(),
        ),
        out_specs=(
            P("ctx", "kv", None),
            P("ctx", "kv", None),
            P("ctx", "kv", None),
            P("ctx", None, None),
        ),
        check_vma=False,
    )
```

profile of v0, /device:TPU:0, one launch (start us, length us, event | category | flops | bytes accessed | tf_op | source)
XLA Modules:
  0.0 130.0 jit_solution(4736945135432841104)
XLA Ops:
  0.6 3.4 %collective-permute-start.1 = (f32[128,128]{1,0:T(8,128)}, f32[128,128]{1,0:T(8,128)S(1)}, u32[]{:S(2)}, u32[]{:S(2)}) collective-permute-start(f32[128,128]{1,0:T(8,128)} %bitcast.269), channel_id=1, source_target_pairs={{0,28},{4,0},{8,4},{12,8},{16,12},{20,16},{24,20},{28,24},{1,29},{... | collective-permute-start | bytes 196616 | tf_op jit(solution)/shard_map/ppermute | solution.py:21
  5.3 1.6 %copy.50 = bf16[384,2,128]{2,0,1:T(8,128)(2,1)} copy(bf16[384,2,128]{2,1,0:T(2,128)(2,1)} %param.8) | data formatting | bytes 393216 | tf_op args[1]
  7.0 1.9 %fusion.54 = f32[2,384,128]{2,1,0:T(8,128)} fusion(f32[1,128,128]{2,1,0:T(8,128)} %param.11, bf16[384,2,128]{2,1,0:T(2,128)(2,1)} %param.8), kind=kOutput, calls=%fused_computation.114 | convolution fusion | flops 25182208 | bytes 655360 | tf_op jit(solution)/shard_map/gld,ed->gle/dot_general | solution.py:32
  9.0 1.3 copy-done.6
  10.3 1.2 copy_bitcast_fusion.2
  13.8 1.6 %slice_bitcast_fusion.2 = (bf16[3072,128]{1,0:T(8,128)(2,1)S(1)}, bf16[3072,128]{1,0:T(8,128)(2,1)S(1)}, bf16[3072,128]{1,0:T(8,128)(2,1)S(1)}, bf16[3072,128]{1,0:T(8,128)(2,1)S(1)}) fusion(bf16[2,384,8,128]{3,2,1,0:T(8,128)(2,1)S(1)} %copy_bitcast_fusion.1, bf16[2,384,8,128]{3,2,1,0:T(8,128)(2,1)} %copy_bitcast_fusion.2), kind=kLoop, calls=%fused_computation.33 | loop fusion | bytes 6291456 | tf_op jit(solution)/shard_map/squeeze | solution.py:192
  17.4 1.3 collective-permute-start.2
  18.7 1.3 %collective-permute-start.4 = (bf16[2,384,128]{2,1,0:T(8,128)(2,1)S(1)}, bf16[2,384,128]{2,1,0:T(8,128)(2,1)S(1)}, u32[]{:S(2)}, u32[]{:S(2)}) collective-permute-start(bf16[2,384,128]{2,1,0:T(8,128)(2,1)S(1)} %get-tuple-element.40), channel_id=1, source_target_pairs={{0,12},{4,16},{8,20},{12,24},{16,28},{20,0},{24,4},{28,8},{1,13},{... | collective-permute-start | bytes 589832 | tf_op jit(solution)/shard_map/ppermute | solution.py:21
  20.8 1.6 %collective-permute-start.6 = (bf16[2,384,128]{2,1,0:T(8,128)(2,1)S(1)}, bf16[2,384,128]{2,1,0:T(8,128)(2,1)S(1)}, u32[]{:S(2)}, u32[]{:S(2)}) collective-permute-start(bf16[2,384,128]{2,1,0:T(8,128)(2,1)S(1)} %get-tuple-element.46), channel_id=1, source_target_pairs={{0,8},{4,12},{8,16},{12,20},{16,24},{20,28},{24,0},{28,4},{1,9},{5... | collective-permute-start | bytes 589832 | tf_op jit(solution)/shard_map/ppermute | solution.py:21
  22.4 2.3 %collective-permute-done.refs_4_ = bf16[2,384,128]{2,1,0:T(8,128)(2,1)S(1)} collective-permute-done((bf16[2,384,128]{2,1,0:T(8,128)(2,1)S(1)}, bf16[2,384,128]{2,1,0:T(8,128)(2,1)S(1)}, u32[]{:S(2)}, u32[]{:S(2)}) %collective-permute-start) | collective-permute-done | bytes 196640 | tf_op jit(solution)/shard_map/ppermute | solution.py:21
  24.8 1.4 %collective-permute-done.2.refs_5_ = bf16[2,384,128]{2,1,0:T(8,128)(2,1)S(1)} collective-permute-done((bf16[2,384,128]{2,1,0:T(8,128)(2,1)S(1)}, bf16[2,384,128]{2,1,0:T(8,128)(2,1)S(1)}, u32[]{:S(2)}, u32[]{:S(2)}) %collective-permute-start.2) | collective-permute-done | bytes 196640 | tf_op jit(solution)/shard_map/ppermute | solution.py:21
  26.2 14.0 %collective-permute-done.4.refs_6_ = bf16[2,384,128]{2,1,0:T(8,128)(2,1)S(1)} collective-permute-done((bf16[2,384,128]{2,1,0:T(8,128)(2,1)S(1)}, bf16[2,384,128]{2,1,0:T(8,128)(2,1)S(1)}, u32[]{:S(2)}, u32[]{:S(2)}) %collective-permute-start.4) | collective-permute-done | bytes 196640 | tf_op jit(solution)/shard_map/ppermute | solution.py:21
  40.1 25.3 %shard_map.102 = (bf16[3072,128]{1,0:T(8,128)(2,1)S(1)}, bf16[1536,128]{1,0:T(8,128)(2,1)S(1)}, bf16[1536,128]{1,0:T(8,128)(2,1)S(1)}) custom-call(s32[1]{0:T(128)} %get-tuple-element.48.refs_0_, bf16[3072,128]{1,0:T(8,128)(2,1)S(1)} %get-tuple-element.55.refs_1_, bf16[3072,128]{1,0:T(8,128)(2,1)S(1)} %get-tuple-element.20.refs_2_, ...), custom_call_target="tpu_custom_call" | custom-call | flops 6039797760 | bytes 3932160 | tf_op jit(solution)/shard_map/pallas_call | solution.py:138
  65.6 18.8 %shard_map.103 = (bf16[3072,128]{1,0:T(8,128)(2,1)S(1)}, bf16[1536,128]{1,0:T(8,128)(2,1)S(1)}, bf16[1536,128]{1,0:T(8,128)(2,1)S(1)}) custom-call(s32[1]{0:T(128)} %get-tuple-element.49.refs_0_, bf16[3072,128]{1,0:T(8,128)(2,1)S(1)} %get-tuple-element.54.refs_1_, bf16[3072,128]{1,0:T(8,128)(2,1)S(1)} %get-tuple-element.21.refs_2_, ...), custom_call_target="tpu_custom_call" | custom-call | flops 6039797760 | bytes 3932160 | tf_op jit(solution)/shard_map/pallas_call | solution.py:138
  84.4 1.7 %collective-permute-start.11 = (bf16[2,384,128]{2,1,0:T(8,128)(2,1)S(1)}, bf16[2,384,128]{2,1,0:T(8,128)(2,1)S(1)}, u32[]{:S(2)}, u32[]{:S(2)}) collective-permute-start(bf16[2,384,128]{2,1,0:T(8,128)(2,1)S(1)} %get-tuple-element.29), channel_id=1, source_target_pairs={{0,28},{4,0},{8,4},{12,8},{16,12},{20,16},{24,20},{28,24},{1,29},{... | collective-permute-start | bytes 589832 | tf_op jit(solution)/shard_map/ppermute | solution.py:21
  86.1 1.3 %collective-permute-start.13 = (bf16[2,384,128]{2,1,0:T(8,128)(2,1)S(1)}, bf16[2,384,128]{2,1,0:T(8,128)(2,1)S(1)}, u32[]{:S(2)}, u32[]{:S(2)}) collective-permute-start(bf16[2,384,128]{2,1,0:T(8,128)(2,1)S(1)} %get-tuple-element.27), channel_id=1, source_target_pairs={{0,20},{4,24},{8,28},{12,0},{16,4},{20,8},{24,12},{28,16},{1,21},{... | collective-permute-start | bytes 589832 | tf_op jit(solution)/shard_map/ppermute | solution.py:21
  87.4 1.4 %collective-permute-start.8 = (bf16[2,384,128]{2,1,0:T(8,128)(2,1)S(1)}, bf16[2,384,128]{2,1,0:T(8,128)(2,1)S(1)}, u32[]{:S(2)}, u32[]{:S(2)}) collective-permute-start(bf16[2,384,128]{2,1,0:T(8,128)(2,1)S(1)} %get-tuple-element.26), channel_id=1, source_target_pairs={{0,28},{4,0},{8,4},{12,8},{16,12},{20,16},{24,20},{28,24},{1,29},{... | collective-permute-start | bytes 589832 | tf_op jit(solution)/shard_map/ppermute | solution.py:21
  88.8 1.4 %copy_bitcast_fusion = bf16[384,16,128]{2,1,0:T(8,128)(2,1)} fusion(bf16[1,384,8,128]{3,2,1,0:T(8,128)(2,1)S(1)} %bitcast.260, bf16[1,384,8,128]{3,2,1,0:T(8,128)(2,1)S(1)} %bitcast.259), kind=kLoop, calls=%fused_computation.1 | loop fusion | flops 786432 | bytes 3145728 | tf_op jit(solution)/shard_map/reshape | solution.py:211
  90.3 1.9 %collective-permute-start.9 = (bf16[2,384,128]{2,1,0:T(8,128)(2,1)S(1)}, bf16[2,384,128]{2,1,0:T(8,128)(2,1)S(1)}, u32[]{:S(2)}, u32[]{:S(2)}) collective-permute-start(bf16[2,384,128]{2,1,0:T(8,128)(2,1)S(1)} %get-tuple-element.25), channel_id=1, source_target_pairs={{0,24},{4,28},{8,0},{12,4},{16,8},{20,12},{24,16},{28,20},{1,25},{... | collective-permute-start | bytes 589832 | tf_op jit(solution)/shard_map/ppermute | solution.py:21
  92.4 9.1 %collective-permute-done.9 = bf16[2,384,128]{2,1,0:T(8,128)(2,1)S(1)} collective-permute-done((bf16[2,384,128]{2,1,0:T(8,128)(2,1)S(1)}, bf16[2,384,128]{2,1,0:T(8,128)(2,1)S(1)}, u32[]{:S(2)}, u32[]{:S(2)}) %collective-permute-start.9) | collective-permute-done | bytes 196640 | tf_op jit(solution)/shard_map/ppermute | solution.py:21
  103.9 3.5 %collective-permute-start.15 = (bf16[128,128]{1,0:T(8,128)(2,1)S(1)}, bf16[128,128]{1,0:T(8,128)(2,1)S(1)}, u32[]{:S(2)}, u32[]{:S(2)}) collective-permute-start(bf16[128,128]{1,0:T(8,128)(2,1)S(1)} %fusion.13), channel_id=1, source_target_pairs={{0,8},{4,12},{8,16},{12,20},{16,24},{20,28},{24,0},{28,4},{1,9},{5... | collective-permute-start | bytes 98312 | tf_op jit(solution)/shard_map/ppermute | solution.py:21
  107.6 0.9 collective-permute-start.14
  110.8 1.1 collective-permute-done.14
  112.1 17.2 %psum.7 = bf16[1,128,128]{2,1,0:T(8,128)(2,1)S(1)} all-reduce(bf16[1,128,128]{2,1,0:T(8,128)(2,1)S(1)} %fusion.38), channel_id=1, replica_groups=mesh['ctx'=8,'kv'=4] {'kv'}, use_global_device_ids=true, to_apply=%region_0.1 | all-reduce | flops 16384 | bytes 65536 | tf_op jit(solution)/shard_map/psum | solution.py:209
  (85 shorter events, 11.5 us)
Async XLA Ops:
  0.6 8.2 %copy-start = (bf16[384,16,128]{2,1,0:T(8,128)(2,1)S(1)}, bf16[384,16,128]{2,1,0:T(8,128)(2,1)}, u32[]{:S(2)}) copy-start(bf16[384,16,128]{2,1,0:T(8,128)(2,1)} %param.10) | copy-start | bytes 4718596
  0.6 14.9 %collective-permute-start.1 = (f32[128,128]{1,0:T(8,128)}, f32[128,128]{1,0:T(8,128)S(1)}, u32[]{:S(2)}, u32[]{:S(2)}) collective-permute-start(f32[128,128]{1,0:T(8,128)} %bitcast.269), channel_id=1, source_target_pairs={{0,28},{4,0},{8,4},{12,8},{16,12},{20,16},{24,20},{28,24},{1,29},{... | collective-permute-start | bytes 196616 | tf_op jit(solution)/shard_map/ppermute | solution.py:21
  4.0 11.9 %collective-permute-start.3 = (f32[128,128]{1,0:T(8,128)}, f32[128,128]{1,0:T(8,128)S(1)}, u32[]{:S(2)}, u32[]{:S(2)}) collective-permute-start(f32[128,128]{1,0:T(8,128)} %bitcast.270), channel_id=1, source_target_pairs={{0,24},{4,28},{8,0},{12,4},{16,8},{20,12},{24,16},{28,20},{1,25},{... | collective-permute-start | bytes 196616 | tf_op jit(solution)/shard_map/ppermute | solution.py:21
  10.3 2.0 %copy-start.1 = (bf16[384,2,128]{2,1,0:T(2,128)(2,1)S(1)}, bf16[384,2,128]{2,1,0:T(2,128)(2,1)}, u32[]{:S(2)}) copy-start(bf16[384,2,128]{2,1,0:T(2,128)(2,1)} %param.8) | copy-start | bytes 589828
  10.3 2.0 %copy-start.2 = (f32[1,128,128]{2,1,0:T(8,128)S(1)}, f32[1,128,128]{2,1,0:T(8,128)}, u32[]{:S(2)}) copy-start(f32[1,128,128]{2,1,0:T(8,128)} %param.11) | copy-start | bytes 196612
  10.3 2.0 %copy-start.7 = (f32[2,384,128]{2,1,0:T(8,128)S(1)}, f32[2,384,128]{2,1,0:T(8,128)}, u32[]{:S(2)}) copy-start(f32[2,384,128]{2,1,0:T(8,128)} %fusion.54) | copy-start | bytes 1179652
  13.8 1.6 %copy-start.8 = (bf16[384,2,128]{2,0,1:T(8,128)(2,1)S(1)}, bf16[384,2,128]{2,0,1:T(8,128)(2,1)}, u32[]{:S(2)}) copy-start(bf16[384,2,128]{2,0,1:T(8,128)(2,1)} %copy.49) | copy-start | bytes 589828
  13.8 1.7 %copy-start.12 = (s32[2]{0:T(128)S(1)}, s32[2]{0:T(128)}, u32[]{:S(2)}) copy-start(s32[2]{0:T(128)} %param.12) | copy-start | bytes 28
  16.7 4.0 %copy-start.9 = (bf16[1,384,128]{2,1,0:T(8,128)(2,1)S(1)}, bf16[1,384,128]{2,1,0:T(8,128)(2,1)}, u32[]{:S(2)}) copy-start(bf16[1,384,128]{2,1,0:T(8,128)(2,1)} %get-tuple-element.35) | copy-start | bytes 294916
  17.2 7.5 %collective-permute-start = (bf16[2,384,128]{2,1,0:T(8,128)(2,1)S(1)}, bf16[2,384,128]{2,1,0:T(8,128)(2,1)S(1)}, u32[]{:S(2)}, u32[]{:S(2)}) collective-permute-start(bf16[2,384,128]{2,1,0:T(8,128)(2,1)S(1)} %get-tuple-element.41), channel_id=1, source_target_pairs={{0,4},{4,8},{8,12},{12,16},{16,20},{20,24},{24,28},{28,0},{1,5},{5... | collective-permute-start | bytes 589832 | tf_op jit(solution)/shard_map/ppermute | solution.py:21
  17.4 8.7 %collective-permute-start.2 = (bf16[2,384,128]{2,1,0:T(8,128)(2,1)S(1)}, bf16[2,384,128]{2,1,0:T(8,128)(2,1)S(1)}, u32[]{:S(2)}, u32[]{:S(2)}) collective-permute-start(bf16[2,384,128]{2,1,0:T(8,128)(2,1)S(1)} %get-tuple-element.42), channel_id=1, source_target_pairs={{0,8},{4,12},{8,16},{12,20},{16,24},{20,28},{24,0},{28,4},{1,9},{5... | collective-permute-start | bytes 589832 | tf_op jit(solution)/shard_map/ppermute | solution.py:21
  18.7 21.4 %collective-permute-start.4 = (bf16[2,384,128]{2,1,0:T(8,128)(2,1)S(1)}, bf16[2,384,128]{2,1,0:T(8,128)(2,1)S(1)}, u32[]{:S(2)}, u32[]{:S(2)}) collective-permute-start(bf16[2,384,128]{2,1,0:T(8,128)(2,1)S(1)} %get-tuple-element.40), channel_id=1, source_target_pairs={{0,12},{4,16},{8,20},{12,24},{16,28},{20,0},{24,4},{28,8},{1,13},{... | collective-permute-start | bytes 589832 | tf_op jit(solution)/shard_map/ppermute | solution.py:21
  20.7 44.8 %collective-permute-start.5 = (bf16[2,384,128]{2,1,0:T(8,128)(2,1)S(1)}, bf16[2,384,128]{2,1,0:T(8,128)(2,1)S(1)}, u32[]{:S(2)}, u32[]{:S(2)}) collective-permute-start(bf16[2,384,128]{2,1,0:T(8,128)(2,1)S(1)} %get-tuple-element.45), channel_id=1, source_target_pairs={{0,4},{4,8},{8,12},{12,16},{16,20},{20,24},{24,28},{28,0},{1,5},{5... | collective-permute-start | bytes 589832 | tf_op jit(solution)/shard_map/ppermute | solution.py:21
  20.8 44.8 %collective-permute-start.6 = (bf16[2,384,128]{2,1,0:T(8,128)(2,1)S(1)}, bf16[2,384,128]{2,1,0:T(8,128)(2,1)S(1)}, u32[]{:S(2)}, u32[]{:S(2)}) collective-permute-start(bf16[2,384,128]{2,1,0:T(8,128)(2,1)S(1)} %get-tuple-element.46), channel_id=1, source_target_pairs={{0,8},{4,12},{8,16},{12,20},{16,24},{20,28},{24,0},{28,4},{1,9},{5... | collective-permute-start | bytes 589832 | tf_op jit(solution)/shard_map/ppermute | solution.py:21
  24.8 40.8 %collective-permute-start.7 = (bf16[2,384,128]{2,1,0:T(8,128)(2,1)S(1)}, bf16[2,384,128]{2,1,0:T(8,128)(2,1)S(1)}, u32[]{:S(2)}, u32[]{:S(2)}) collective-permute-start(bf16[2,384,128]{2,1,0:T(8,128)(2,1)S(1)} %get-tuple-element.44), channel_id=1, source_target_pairs={{0,12},{4,16},{8,20},{12,24},{16,28},{20,0},{24,4},{28,8},{1,13},{... | collective-permute-start | bytes 589832 | tf_op jit(solution)/shard_map/ppermute | solution.py:21
  65.5 24.8 %collective-permute-start.10 = (bf16[2,384,128]{2,1,0:T(8,128)(2,1)S(1)}, bf16[2,384,128]{2,1,0:T(8,128)(2,1)S(1)}, u32[]{:S(2)}, u32[]{:S(2)}) collective-permute-start(bf16[2,384,128]{2,1,0:T(8,128)(2,1)S(1)} %get-tuple-element.24), channel_id=1, source_target_pairs={{0,20},{4,24},{8,28},{12,0},{16,4},{20,8},{24,12},{28,16},{1,21},{... | collective-permute-start | bytes 589832 | tf_op jit(solution)/shard_map/ppermute | solution.py:21
  84.4 18.7 %collective-permute-start.11 = (bf16[2,384,128]{2,1,0:T(8,128)(2,1)S(1)}, bf16[2,384,128]{2,1,0:T(8,128)(2,1)S(1)}, u32[]{:S(2)}, u32[]{:S(2)}) collective-permute-start(bf16[2,384,128]{2,1,0:T(8,128)(2,1)S(1)} %get-tuple-element.29), channel_id=1, source_target_pairs={{0,28},{4,0},{8,4},{12,8},{16,12},{20,16},{24,20},{28,24},{1,29},{... | collective-permute-start | bytes 589832 | tf_op jit(solution)/shard_map/ppermute | solution.py:21
  86.1 16.4 %collective-permute-start.12 = (bf16[2,384,128]{2,1,0:T(8,128)(2,1)S(1)}, bf16[2,384,128]{2,1,0:T(8,128)(2,1)S(1)}, u32[]{:S(2)}, u32[]{:S(2)}) collective-permute-start(bf16[2,384,128]{2,1,0:T(8,128)(2,1)S(1)} %get-tuple-element.28), channel_id=1, source_target_pairs={{0,24},{4,28},{8,0},{12,4},{16,8},{20,12},{24,16},{28,20},{1,25},{... | collective-permute-start | bytes 589832 | tf_op jit(solution)/shard_map/ppermute | solution.py:21
  86.1 16.0 %collective-permute-start.13 = (bf16[2,384,128]{2,1,0:T(8,128)(2,1)S(1)}, bf16[2,384,128]{2,1,0:T(8,128)(2,1)S(1)}, u32[]{:S(2)}, u32[]{:S(2)}) collective-permute-start(bf16[2,384,128]{2,1,0:T(8,128)(2,1)S(1)} %get-tuple-element.27), channel_id=1, source_target_pairs={{0,20},{4,24},{8,28},{12,0},{16,4},{20,8},{24,12},{28,16},{1,21},{... | collective-permute-start | bytes 589832 | tf_op jit(solution)/shard_map/ppermute | solution.py:21
  87.4 14.4 %collective-permute-start.8 = (bf16[2,384,128]{2,1,0:T(8,128)(2,1)S(1)}, bf16[2,384,128]{2,1,0:T(8,128)(2,1)S(1)}, u32[]{:S(2)}, u32[]{:S(2)}) collective-permute-start(bf16[2,384,128]{2,1,0:T(8,128)(2,1)S(1)} %get-tuple-element.26), channel_id=1, source_target_pairs={{0,28},{4,0},{8,4},{12,8},{16,12},{20,16},{24,20},{28,24},{1,29},{... | collective-permute-start | bytes 589832 | tf_op jit(solution)/shard_map/ppermute | solution.py:21
  90.3 11.2 %collective-permute-start.9 = (bf16[2,384,128]{2,1,0:T(8,128)(2,1)S(1)}, bf16[2,384,128]{2,1,0:T(8,128)(2,1)S(1)}, u32[]{:S(2)}, u32[]{:S(2)}) collective-permute-start(bf16[2,384,128]{2,1,0:T(8,128)(2,1)S(1)} %get-tuple-element.25), channel_id=1, source_target_pairs={{0,24},{4,28},{8,0},{12,4},{16,8},{20,12},{24,16},{28,20},{1,25},{... | collective-permute-start | bytes 589832 | tf_op jit(solution)/shard_map/ppermute | solution.py:21
  92.3 10.5 %copy-start.5 = (bf16[2,384,128]{2,1,0:T(8,128)(2,1)S(1)}, bf16[2,384,128]{2,1,0:T(8,128)(2,1)}, u32[]{:S(2)}) copy-start(bf16[2,384,128]{2,1,0:T(8,128)(2,1)} %copy-done.4) | copy-start | bytes 589828
  103.9 7.0 %collective-permute-start.15 = (bf16[128,128]{1,0:T(8,128)(2,1)S(1)}, bf16[128,128]{1,0:T(8,128)(2,1)S(1)}, u32[]{:S(2)}, u32[]{:S(2)}) collective-permute-start(bf16[128,128]{1,0:T(8,128)(2,1)S(1)} %fusion.13), channel_id=1, source_target_pairs={{0,8},{4,12},{8,16},{12,20},{16,24},{20,28},{24,0},{28,4},{1,9},{5... | collective-permute-start | bytes 98312 | tf_op jit(solution)/shard_map/ppermute | solution.py:21
  107.6 4.3 %collective-permute-start.14 = (bf16[128,128]{1,0:T(8,128)(2,1)S(1)}, bf16[128,128]{1,0:T(8,128)(2,1)S(1)}, u32[]{:S(2)}, u32[]{:S(2)}) collective-permute-start(bf16[128,128]{1,0:T(8,128)(2,1)S(1)} %fusion.12), channel_id=1, source_target_pairs={{0,4},{4,8},{8,12},{12,16},{16,20},{20,24},{24,28},{28,0},{1,5},{5... | collective-permute-start | bytes 98312 | tf_op jit(solution)/shard_map/ppermute | solution.py:21
  (5 other events, 5.9 us)
where the time goes:
time: 133 us; the launch traced here: 130 us
  Pallas kernels  44 us (33%)
  waiting for transfers between devices  27.9 us (21%)
  starting transfers between devices  19.5 us (15%)
  blocking collectives  17.2 us (13%)
  local copies, waits for them, and re-layouts  10.6 us (8%)
  matrix products  6.57 us (5%)
  other arithmetic  2.44 us (2%)
  between operations  1.74 us (1%)
    pallas_call x2, Pallas kernels, attention(): pl.pallas_call(lambda *refs: attention_kernel(groups, factor, *refs), gri...  44 us
    ppermute x16, waiting for transfers between devices, passed_along(): lax.ppermute(shard, 'ctx', [(i, (i + by) % peers) for i in range(peers)])  27.9 us
    ppermute x16, starting transfers between devices, passed_along(): lax.ppermute(shard, 'ctx', [(i, (i + by) % peers) for i in range(peers)])  19.5 us
    psum x1, blocking collectives, shards(): turn_total = lax.psum(turn_total.astype(HALF), 'kv').astype(FULL)  17.2 us
    unnamed x30, local copies, waits for them, and re-layouts  6.32 us
    dot_general x9, matrix products, times_split(): first = jnp.einsum(spec, rows_half, upper, preferred_element_type=FULL)  3.24 us
  transfers between devices with their start and end apart: 16, of which 5 were waited for; matrix products, arithmetic and copies ran while one was open for 11% of the time, Pallas kernels for 34%

commit v1 on v0

--- a/solution.py
+++ b/solution.py
@@ -33,9 +33,11 @@
     return first + jnp.einsum(spec, rows_half, lower, preferred_element_type=FULL)
 
 
-def attention_kernel(groups, factor, hops_ref, q_ref, g_ref, *refs):
+def attention_kernel(groups, factor, hops_ref, turn_ref, q_ref, g_ref, *refs):
     kv_refs = refs[: HOPS + 1]
-    dq_ref, dk_ref, dv_ref, e_ref, slope_ref, max_ref, dk_acc, dv_acc, dq_acc = refs[HOPS + 1 :]
+    dq_ref, dk_ref, dv_ref, e_ref, slope_ref, max_ref, dk_acc, dv_acc, dq_acc, tile_ref = (
+        refs[HOPS + 1 :]
+    )
     tile = pl.program_id(0)
     tiles = pl.num_programs(0)
     rows = q_ref.shape[0]
@@ -47,6 +49,12 @@
     def _():
         dk_acc[...] = jnp.zeros_like(dk_acc)
         dv_acc[...] = jnp.zeros_like(dv_acc)
+        tile_ref[0] = kv_refs[0][0]
+        for hop in range(1, HOPS + 1):
+            keys = kv_refs[hop][0]
+            first = lax.dot_general(keys, turn_ref[hop - 1, 0], NT, preferred_element_type=FULL)
+            second = lax.dot_general(keys, turn_ref[hop - 1, 1], NT, preferred_element_type=FULL)
+            tile_ref[hop] = (first + second).astype(HALF)
 
     def forward(keys, values, slot, state, masked):
         top, total, dot = state
@@ -86,11 +94,11 @@
         jnp.zeros((1, rows), FULL),
     )
     own = kv_refs[0]
-    state = forward(own[0, spot_of(tile), :], own[1, spot_of(tile), :], tile, state, True)
+    state = forward(tile_ref[0, spot_of(tile), :], own[1, spot_of(tile), :], tile, state, True)
     state = lax.fori_loop(
         0,
         tile,
-        lambda i, s: forward(own[0, spot_of(i), :], own[1, spot_of(i), :], i, s, False),
+        lambda i, s: forward(tile_ref[0, spot_of(i), :], own[1, spot_of(i), :], i, s, False),
         state,
     )
     for hop in range(1, HOPS + 1):
@@ -99,7 +107,11 @@
             0,
             jnp.where(hop < hop_count, per_hop, 0),
             lambda i, s, ref=ref, hop=hop: forward(
-                ref[0, spot_of(i), :], ref[1, spot_of(i), :], hop * per_hop + i, s, False
+                tile_ref[hop, spot_of(i), :],
+                ref[1, spot_of(i), :],
+                hop * per_hop + i,
+                s,
+                False,
             ),
             state,
         )
@@ -108,11 +120,10 @@
     final = (top, inverse, dot * inverse)
     dq_acc[...] = jnp.zeros_like(dq_acc)
     for hop in range(HOPS + 1):
-        ref = kv_refs[hop]
         trips = tile + 1 if hop == 0 else jnp.where(hop < hop_count, per_hop, 0)
 
-        def step(i, carry, ref=ref, hop=hop):
-            backward(ref[0, spot_of(i), :], hop * per_hop + i, final)
+        def step(i, carry, hop=hop):
+            backward(tile_ref[hop, spot_of(i), :], hop * per_hop + i, final)
             return carry
 
         lax.fori_loop(0, trips, step, 0)
@@ -124,7 +135,7 @@
         dv_ref[...] = dv_acc[...].astype(HALF)
 
 
-def attention(hop_count, query_rows, grad_rows, pairs, groups, factor):
+def attention(hop_count, turn_parts, query_rows, grad_rows, pairs, groups, factor):
     total_rows, width = query_rows.shape
     length = pairs[0].shape[1]
     tiles = length // CHUNK
@@ -138,7 +149,12 @@
     return pl.pallas_call(
         lambda *refs: attention_kernel(groups, factor, *refs),
         grid=(tiles,),
-        in_specs=[pl.BlockSpec(memory_space=pltpu.SMEM), row_spec, row_spec]
+        in_specs=[
+            pl.BlockSpec(memory_space=pltpu.SMEM),
+            pl.BlockSpec(turn_parts.shape, lambda i: (0, 0, 0, 0)),
+            row_spec,
+            row_spec,
+        ]
         + [pl.BlockSpec((2, length, width), whole)] * hops,
         out_specs=[row_spec, part_spec, part_spec],
         out_shape=[
@@ -153,6 +169,7 @@
             pltpu.VMEM((keys, width), FULL),
             pltpu.VMEM((keys, width), FULL),
             pltpu.VMEM((width, rows), FULL),
+            pltpu.VMEM((hops, length, width), HALF),
         ],
         compiler_params=pltpu.CompilerParams(vmem_limit_bytes=40 * 1024 * 1024),
         cost_estimate=pl.CostEstimate(
@@ -160,7 +177,7 @@
             bytes_accessed=6 * total_rows * width + 8 * keys * width,
             transcendentals=total_rows * keys,
         ),
-    )(hop_count, query_rows, grad_rows, *pairs)
+    )(hop_count, turn_parts, query_rows, grad_rows, *pairs)
 
 
 def shards(queries, key_heads, value_heads, grad_out, transforms, window, first_block):
@@ -171,12 +188,22 @@
     blocks = lax.axis_size("ctx")
     position = (lax.axis_index("ctx") - first_block[0]) % blocks
     hop_counts = jnp.minimum(window, position + 1)
+    pairs = [
+        [jnp.stack([key_heads[:, g], value_heads[:, g]])] for g in range(kv_heads)
+    ]
+    arriving = [passed_along(transforms[0], h) for h in range(1, HOPS + 1)]
+    for g in range(kv_heads):
+        for h in range(1, HOPS + 1):
+            pairs[g].append(passed_along(pairs[g][0], h))
+    met = [arriving[0]]
+    for h in range(1, HOPS):
+        met.append(jnp.dot(met[-1], arriving[h], precision=PRECISE))
+    turn_parts = jnp.stack([jnp.stack(split_parts(m)) for m in met])
     turns = [transforms[0]] + [passed_along(transforms[0], -h) for h in range(1, HOPS)]
     chain = [turns[0]]
-    for h in range(1, HOPS):
+    for h in range(1, HOPS - 1):
         chain.append(jnp.dot(turns[h], chain[-1], precision=PRECISE))
     own_keys = key_heads.transpose(1, 0, 2)
-    own_values = value_heads.transpose(1, 0, 2)
     query_rows = queries.reshape(length, kv_heads, groups, width).transpose(1, 0, 2, 3)
     grad_rows = grad_out.reshape(length, kv_heads, groups, width).transpose(1, 0, 2, 3)
     query_rows = query_rows.reshape(kv_heads, length * groups, width)
@@ -185,11 +212,14 @@
     query_parts, key_grads, value_grads = [], [], []
     turn_terms = [jnp.zeros((width, width), FULL) for _ in range(HOPS)]
     for g in range(kv_heads):
-        pairs = [jnp.stack([own_keys[g], own_values[g]])]
-        for h in range(1, HOPS + 1):
-            pairs.append(passed_along(jnp.stack([turned[h][g], own_values[g]]), h))
         dq, dk, dv = attention(
-            hop_counts[g : g + 1], query_rows[g], grad_rows[g], pairs, groups, factor
+            hop_counts[g : g + 1],
+            turn_parts,
+            query_rows[g],
+            grad_rows[g],
+            pairs[g],
+            groups,
+            factor,
         )
         query_parts.append(dq)
         back = jnp.stack([dk, dv]).reshape(2, HOPS + 1, length, width)

time: 133 us -> 130 us (0.977); the launches traced: 130 us -> 129 us
  waiting for transfers between devices: 27.9 us -> 15.9 us
  matrix products: 6.57 us -> 12.2 us
  blocking collectives: 17.2 us -> 19.3 us
    ppermute x16 -> x19, waiting for transfers between devices: 27.9 us -> 15.9 us  [passed_along(): lax.ppermute(shard, 'ctx', [(i, (i + by) % peers) for i in range(peers)])]
    dot_general x9 -> x8, matrix products: 1.57 us -> 3.89 us  [times_split(): jnp.einsum(spec, rows_half, lower, preferred_element_type=FULL)]
    dot_general x0 -> x2, matrix products: none -> 2.11 us  [shards(): met.append(jnp.dot(met[-1], arriving[h], precision=PRECISE))]
    psum x1, blocking collectives: 17.2 us -> 19.3 us  [shards(): turn_total = lax.psum(turn_total.astype(HALF), 'kv').astype(FULL)]
    unnamed x30 -> x37, local copies, waits for them, and re-layouts: 6.32 us -> 4.78 us
    ppermute x16 -> x19, starting transfers between devices: 19.5 us -> 20.5 us  [passed_along(): lax.ppermute(shard, 'ctx', [(i, (i + by) % peers) for i in range(peers)])]
    dot_general x9 -> x8, matrix products: 3.24 us -> 3.86 us  [times_split(): first = jnp.einsum(spec, rows_half, upper, preferred_element_type=FULL)]
  transfers between devices with their start and end apart: 16 -> 19, of which waited for: 5 -> 3; matrix products, arithmetic and copies ran while one was open for 11% -> 18% of each run, Pallas kernels for 34% -> 35%
where the time goes in v1:
time: 130 us; the launch traced here: 129 us
  Pallas kernels  44.6 us (34%)
  starting transfers between devices  20.5 us (16%)
  blocking collectives  19.3 us (15%)
  waiting for transfers between devices  15.9 us (12%)
  matrix products  12.2 us (9%)
  local copies, waits for them, and re-layouts  11.1 us (9%)
  other arithmetic  3.35 us (3%)
  between operations  1.8 us (1%)
    pallas_call x2, Pallas kernels, attention(): pl.pallas_call(lambda *refs: attention_kernel(groups, factor, *refs), gri...  44.6 us
    ppermute x19, starting transfers between devices, passed_along(): lax.ppermute(shard, 'ctx', [(i, (i + by) % peers) for i in range(peers)])  20.5 us
    psum x1, blocking collectives, shards(): turn_total = lax.psum(turn_total.astype(HALF), 'kv').astype(FULL)  19.3 us
    ppermute x19, waiting for transfers between devices, passed_along(): lax.ppermute(shard, 'ctx', [(i, (i + by) % peers) for i in range(peers)])  15.9 us
    unnamed x37, local copies, waits for them, and re-layouts  4.78 us
    dot_general x8, matrix products, times_split(): jnp.einsum(spec, rows_half, lower, preferred_element_type=FULL)  3.89 us
    dot_general x8, matrix products, times_split(): first = jnp.einsum(spec, rows_half, upper, preferred_element_type=FULL)  3.86 us
  transfers between devices with their start and end apart: 19, of which 3 were waited for; matrix products, arithmetic and copies ran while one was open for 18% of the time, Pallas kernels for 35%

profile of v1, /device:TPU:0, one launch (start us, length us, event | category | flops | bytes accessed | tf_op | source)
XLA Modules:
  0.0 128.6 jit_solution(39067502707920114)
XLA Ops:
  1.2 2.6 %collective-permute-start.1 = (f32[128,128]{1,0:T(8,128)}, f32[128,128]{1,0:T(8,128)}, u32[]{:S(2)}, u32[]{:S(2)}) collective-permute-start(f32[128,128]{1,0:T(8,128)} %bitcast.289), channel_id=1, source_target_pairs={{0,8},{4,12},{8,16},{12,20},{16,24},{20,28},{24,0},{28,4},{1,9},{5... | collective-permute-start | bytes 196616 | tf_op jit(solution)/shard_map/ppermute | solution.py:21
  3.7 2.4 %collective-permute-start.2 = (f32[128,128]{1,0:T(8,128)}, f32[128,128]{1,0:T(8,128)}, u32[]{:S(2)}, u32[]{:S(2)}) collective-permute-start(f32[128,128]{1,0:T(8,128)} %bitcast.290), channel_id=1, source_target_pairs={{0,12},{4,16},{8,20},{12,24},{16,28},{20,0},{24,4},{28,8},{1,13},{... | collective-permute-start | bytes 196616 | tf_op jit(solution)/shard_map/ppermute | solution.py:21
  6.4 2.0 %fusion.65 = (bf16[384,1,128]{2,1,0:T(2,128)(2,1)}, bf16[384,1,128]{2,1,0:T(2,128)(2,1)S(1)}) fusion(bf16[384,2,128]{2,1,0:T(2,128)(2,1)} %param.9), kind=kLoop, calls=%fused_computation.140 | loop fusion | bytes 393216 | tf_op jit(solution)/shard_map/slice | solution.py:192
  12.2 1.3 %copy-done.9 = bf16[384,16,128]{2,1,0:T(8,128)(2,1)S(1)} copy-done((bf16[384,16,128]{2,1,0:T(8,128)(2,1)S(1)}, bf16[384,16,128]{2,1,0:T(8,128)(2,1)}, u32[]{:S(2)}) %copy-start.9) | copy-done | bytes 1572888
  13.5 1.2 copy_bitcast_fusion.2
  16.3 1.6 %slice_bitcast_fusion.2 = (bf16[3072,128]{1,0:T(8,128)(2,1)S(1)}, bf16[3072,128]{1,0:T(8,128)(2,1)S(1)}, bf16[3072,128]{1,0:T(8,128)(2,1)S(1)}, bf16[3072,128]{1,0:T(8,128)(2,1)S(1)}) fusion(bf16[2,384,8,128]{3,2,1,0:T(8,128)(2,1)S(1)} %copy_bitcast_fusion.1, bf16[2,384,8,128]{3,2,1,0:T(8,128)(2,1)} %copy_bitcast_fusion.2), kind=kLoop, calls=%fused_computation.29 | loop fusion | bytes 6291456 | tf_op jit(solution)/shard_map/squeeze | solution.py:219
  19.0 1.0 fusion.45
  20.3 2.0 %collective-permute-start.8 = (bf16[2,384,128]{2,1,0:T(8,128)(2,1)S(1)}, bf16[2,384,128]{2,1,0:T(8,128)(2,1)S(1)}, u32[]{:S(2)}, u32[]{:S(2)}) collective-permute-start(bf16[2,384,128]{2,1,0:T(8,128)(2,1)S(1)} %pad_maximum_fusion.4.refs_4_), channel_id=1, source_target_pairs={{0,12},{4,16},{8,20},{12,24},{16,28},{20,0},{24,4},{28,8},{1,13},{... | collective-permute-start | bytes 589832 | tf_op jit(solution)/shard_map/ppermute | solution.py:21
  22.3 1.1 fusion.73
  23.5 1.8 %collective-permute-start.4 = (bf16[2,384,128]{2,1,0:T(8,128)(2,1)S(1)}, bf16[2,384,128]{2,1,0:T(8,128)(2,1)S(1)}, u32[]{:S(2)}, u32[]{:S(2)}) collective-permute-start(bf16[2,384,128]{2,1,0:T(8,128)(2,1)S(1)} %pad_maximum_fusion.3.refs_4_), channel_id=1, source_target_pairs={{0,8},{4,12},{8,16},{12,20},{16,24},{20,28},{24,0},{28,4},{1,9},{5... | collective-permute-start | bytes 589832 | tf_op jit(solution)/shard_map/ppermute | solution.py:21
  25.3 1.0 convert_bitcast_fusion
  27.6 2.1 %collective-permute-start.5 = (bf16[2,384,128]{2,1,0:T(8,128)(2,1)S(1)}, bf16[2,384,128]{2,1,0:T(8,128)(2,1)S(1)}, u32[]{:S(2)}, u32[]{:S(2)}) collective-permute-start(bf16[2,384,128]{2,1,0:T(8,128)(2,1)S(1)} %pad_maximum_fusion.3.refs_4_), channel_id=1, source_target_pairs={{0,12},{4,16},{8,20},{12,24},{16,28},{20,0},{24,4},{28,8},{1,13},{... | collective-permute-start | bytes 589832 | tf_op jit(solution)/shard_map/ppermute | solution.py:21
  30.6 8.9 %collective-permute-done.8.refs_7_ = bf16[2,384,128]{2,1,0:T(8,128)(2,1)S(1)} collective-permute-done((bf16[2,384,128]{2,1,0:T(8,128)(2,1)S(1)}, bf16[2,384,128]{2,1,0:T(8,128)(2,1)S(1)}, u32[]{:S(2)}, u32[]{:S(2)}) %collective-permute-start.8) | collective-permute-done | bytes 196640 | tf_op jit(solution)/shard_map/ppermute | solution.py:21
  39.5 19.0 %shard_map.103 = (bf16[3072,128]{1,0:T(8,128)(2,1)S(1)}, bf16[1536,128]{1,0:T(8,128)(2,1)S(1)}, bf16[1536,128]{1,0:T(8,128)(2,1)S(1)}) custom-call(s32[1]{0:T(128)} %get-tuple-element.47.refs_0_, bf16[3,2,128,128]{3,2,1,0:T(8,128)(2,1)S(1)} %pad_maximum_fusion.2.refs_1_, bf16[3072,128]{1,0:T(8,128)(2,1)S(1)} %get-tuple-element.50.refs_2_, ...), custom_call_target="tpu_custom_call" | custom-call | flops 6039797760 | bytes 3932160 | tf_op jit(solution)/shard_map/pallas_call | solution.py:149
  59.3 25.6 %shard_map.102 = (bf16[3072,128]{1,0:T(8,128)(2,1)S(1)}, bf16[1536,128]{1,0:T(8,128)(2,1)S(1)}, bf16[1536,128]{1,0:T(8,128)(2,1)S(1)}) custom-call(s32[1]{0:T(128)} %get-tuple-element.46.refs_0_, bf16[3,2,128,128]{3,2,1,0:T(8,128)(2,1)S(1)} %pad_maximum_fusion.2.refs_1_, bf16[3072,128]{1,0:T(8,128)(2,1)S(1)} %get-tuple-element.51.refs_2_, ...), custom_call_target="tpu_custom_call" | custom-call | flops 6039797760 | bytes 3932160 | tf_op jit(solution)/shard_map/pallas_call | solution.py:149
  85.0 2.3 %collective-permute-start.9 = (bf16[2,384,128]{2,1,0:T(8,128)(2,1)S(1)}, bf16[2,384,128]{2,1,0:T(8,128)(2,1)S(1)}, u32[]{:S(2)}, u32[]{:S(2)}) collective-permute-start(bf16[2,384,128]{2,1,0:T(8,128)(2,1)S(1)} %get-tuple-element.30), channel_id=1, source_target_pairs={{0,28},{4,0},{8,4},{12,8},{16,12},{20,16},{24,20},{28,24},{1,29},{... | collective-permute-start | bytes 589832 | tf_op jit(solution)/shard_map/ppermute | solution.py:21
  87.3 1.4 %copy_bitcast_fusion = bf16[384,16,128]{2,1,0:T(8,128)(2,1)} fusion(bf16[1,384,8,128]{3,2,1,0:T(8,128)(2,1)S(1)} %bitcast.278, bf16[1,384,8,128]{3,2,1,0:T(8,128)(2,1)S(1)} %bitcast.279), kind=kLoop, calls=%fused_computation.1 | loop fusion | flops 786432 | bytes 3145728 | tf_op jit(solution)/shard_map/reshape | solution.py:241
  89.4 1.1 fusion.55
  90.5 1.0 fusion.17
  91.8 5.0 %collective-permute-done.11 = bf16[2,384,128]{2,1,0:T(8,128)(2,1)S(1)} collective-permute-done((bf16[2,384,128]{2,1,0:T(8,128)(2,1)S(1)}, bf16[2,384,128]{2,1,0:T(8,128)(2,1)S(1)}, u32[]{:S(2)}, u32[]{:S(2)}) %collective-permute-start.11) | collective-permute-done | bytes 196640 | tf_op jit(solution)/shard_map/ppermute | solution.py:21
  97.1 1.1 fusion.56
  100.0 3.6 %collective-permute-start.18 = (bf16[128,128]{1,0:T(8,128)(2,1)S(1)}, bf16[128,128]{1,0:T(8,128)(2,1)S(1)}, u32[]{:S(2)}, u32[]{:S(2)}) collective-permute-start(bf16[128,128]{1,0:T(8,128)(2,1)S(1)} %fusion.11), channel_id=1, source_target_pairs={{0,8},{4,12},{8,16},{12,20},{16,24},{20,28},{24,0},{28,4},{1,9},{5... | collective-permute-start | bytes 98312 | tf_op jit(solution)/shard_map/ppermute | solution.py:21
  106.5 1.9 %collective-permute-done.17 = bf16[128,128]{1,0:T(8,128)(2,1)S(1)} collective-permute-done((bf16[128,128]{1,0:T(8,128)(2,1)S(1)}, bf16[128,128]{1,0:T(8,128)(2,1)S(1)}, u32[]{:S(2)}, u32[]{:S(2)}) %collective-permute-start.17) | collective-permute-done | bytes 32800 | tf_op jit(solution)/shard_map/ppermute | solution.py:21
  108.6 19.3 %psum.7 = bf16[1,128,128]{2,1,0:T(8,128)(2,1)S(1)} all-reduce(bf16[1,128,128]{2,1,0:T(8,128)(2,1)S(1)} %fusion.25), channel_id=1, replica_groups=mesh['ctx'=8,'kv'=4] {'kv'}, use_global_device_ids=true, to_apply=%region_0.1 | all-reduce | flops 16384 | bytes 65536 | tf_op jit(solution)/shard_map/psum | solution.py:239
  (101 shorter events, 16.3 us)
Async XLA Ops:
  0.6 11.4 %copy-start = (bf16[384,16,128]{2,1,0:T(8,128)(2,1)S(1)}, bf16[384,16,128]{2,1,0:T(8,128)(2,1)}, u32[]{:S(2)}) copy-start(bf16[384,16,128]{2,1,0:T(8,128)(2,1)} %param.10) | copy-start | bytes 4718596
  0.6 10.4 %copy-start.4 = (f32[1,128,128]{2,1,0:T(8,128)S(1)}, f32[1,128,128]{2,1,0:T(8,128)}, u32[]{:S(2)}) copy-start(f32[1,128,128]{2,1,0:T(8,128)} %param.11) | copy-start | bytes 196612
  0.7 10.4 %copy-start.1 = (bf16[384,2,128]{2,1,0:T(2,128)(2,1)S(1)}, bf16[384,2,128]{2,1,0:T(2,128)(2,1)}, u32[]{:S(2)}) copy-start(bf16[384,2,128]{2,1,0:T(2,128)(2,1)} %param.8) | copy-start | bytes 589828
  0.7 19.6 %collective-permute-start = (f32[128,128]{1,0:T(8,128)}, f32[128,128]{1,0:T(8,128)}, u32[]{:S(2)}, u32[]{:S(2)}) collective-permute-start(f32[128,128]{1,0:T(8,128)} %bitcast.288), channel_id=1, source_target_pairs={{0,4},{4,8},{8,12},{12,16},{16,20},{20,24},{24,28},{28,0},{1,5},{5... | collective-permute-start | bytes 196616 | tf_op jit(solution)/shard_map/ppermute | solution.py:21
  1.2 21.2 %collective-permute-start.1 = (f32[128,128]{1,0:T(8,128)}, f32[128,128]{1,0:T(8,128)}, u32[]{:S(2)}, u32[]{:S(2)}) collective-permute-start(f32[128,128]{1,0:T(8,128)} %bitcast.289), channel_id=1, source_target_pairs={{0,8},{4,12},{8,16},{12,20},{16,24},{20,28},{24,0},{28,4},{1,9},{5... | collective-permute-start | bytes 196616 | tf_op jit(solution)/shard_map/ppermute | solution.py:21
  3.7 19.7 %collective-permute-start.2 = (f32[128,128]{1,0:T(8,128)}, f32[128,128]{1,0:T(8,128)}, u32[]{:S(2)}, u32[]{:S(2)}) collective-permute-start(f32[128,128]{1,0:T(8,128)} %bitcast.290), channel_id=1, source_target_pairs={{0,12},{4,16},{8,20},{12,24},{16,28},{20,0},{24,4},{28,8},{1,13},{... | collective-permute-start | bytes 196616 | tf_op jit(solution)/shard_map/ppermute | solution.py:21
  6.1 12.5 %collective-permute-start.13 = (f32[128,128]{1,0:T(8,128)}, f32[128,128]{1,0:T(8,128)}, u32[]{:S(2)}, u32[]{:S(2)}) collective-permute-start(f32[128,128]{1,0:T(8,128)} %bitcast.291), channel_id=1, source_target_pairs={{0,28},{4,0},{8,4},{12,8},{16,12},{20,16},{24,20},{28,24},{1,29},{... | collective-permute-start | bytes 196616 | tf_op jit(solution)/shard_map/ppermute | solution.py:21
  10.2 17.4 %collective-permute-start.6 = (bf16[2,384,128]{2,1,0:T(8,128)(2,1)S(1)}, bf16[2,384,128]{2,1,0:T(8,128)(2,1)S(1)}, u32[]{:S(2)}, u32[]{:S(2)}) collective-permute-start(bf16[2,384,128]{2,1,0:T(8,128)(2,1)S(1)} %pad_maximum_fusion.4.refs_4_), channel_id=1, source_target_pairs={{0,4},{4,8},{8,12},{12,16},{16,20},{20,24},{24,28},{28,0},{1,5},{5... | collective-permute-start | bytes 589832 | tf_op jit(solution)/shard_map/ppermute | solution.py:21
  18.6 11.1 %collective-permute-start.7 = (bf16[2,384,128]{2,1,0:T(8,128)(2,1)S(1)}, bf16[2,384,128]{2,1,0:T(8,128)(2,1)S(1)}, u32[]{:S(2)}, u32[]{:S(2)}) collective-permute-start(bf16[2,384,128]{2,1,0:T(8,128)(2,1)S(1)} %pad_maximum_fusion.4.refs_4_), channel_id=1, source_target_pairs={{0,8},{4,12},{8,16},{12,20},{16,24},{20,28},{24,0},{28,4},{1,9},{5... | collective-permute-start | bytes 589832 | tf_op jit(solution)/shard_map/ppermute | solution.py:21
  20.3 19.2 %collective-permute-start.8 = (bf16[2,384,128]{2,1,0:T(8,128)(2,1)S(1)}, bf16[2,384,128]{2,1,0:T(8,128)(2,1)S(1)}, u32[]{:S(2)}, u32[]{:S(2)}) collective-permute-start(bf16[2,384,128]{2,1,0:T(8,128)(2,1)S(1)} %pad_maximum_fusion.4.refs_4_), channel_id=1, source_target_pairs={{0,12},{4,16},{8,20},{12,24},{16,28},{20,0},{24,4},{28,8},{1,13},{... | collective-permute-start | bytes 589832 | tf_op jit(solution)/shard_map/ppermute | solution.py:21
  22.3 36.3 %collective-permute-start.3 = (bf16[2,384,128]{2,1,0:T(8,128)(2,1)S(1)}, bf16[2,384,128]{2,1,0:T(8,128)(2,1)S(1)}, u32[]{:S(2)}, u32[]{:S(2)}) collective-permute-start(bf16[2,384,128]{2,1,0:T(8,128)(2,1)S(1)} %pad_maximum_fusion.3.refs_4_), channel_id=1, source_target_pairs={{0,4},{4,8},{8,12},{12,16},{16,20},{20,24},{24,28},{28,0},{1,5},{5... | collective-permute-start | bytes 589832 | tf_op jit(solution)/shard_map/ppermute | solution.py:21
  23.5 35.9 %collective-permute-start.4 = (bf16[2,384,128]{2,1,0:T(8,128)(2,1)S(1)}, bf16[2,384,128]{2,1,0:T(8,128)(2,1)S(1)}, u32[]{:S(2)}, u32[]{:S(2)}) collective-permute-start(bf16[2,384,128]{2,1,0:T(8,128)(2,1)S(1)} %pad_maximum_fusion.3.refs_4_), channel_id=1, source_target_pairs={{0,8},{4,12},{8,16},{12,20},{16,24},{20,28},{24,0},{28,4},{1,9},{5... | collective-permute-start | bytes 589832 | tf_op jit(solution)/shard_map/ppermute | solution.py:21
  27.6 31.8 %collective-permute-start.5 = (bf16[2,384,128]{2,1,0:T(8,128)(2,1)S(1)}, bf16[2,384,128]{2,1,0:T(8,128)(2,1)S(1)}, u32[]{:S(2)}, u32[]{:S(2)}) collective-permute-start(bf16[2,384,128]{2,1,0:T(8,128)(2,1)S(1)} %pad_maximum_fusion.3.refs_4_), channel_id=1, source_target_pairs={{0,12},{4,16},{8,20},{12,24},{16,28},{20,0},{24,4},{28,8},{1,13},{... | collective-permute-start | bytes 589832 | tf_op jit(solution)/shard_map/ppermute | solution.py:21
  29.7 59.0 %collective-permute-start.12 = (f32[128,128]{1,0:T(8,128)S(1)}, f32[128,128]{1,0:T(8,128)S(1)}, u32[]{:S(2)}, u32[]{:S(2)}) collective-permute-start(f32[128,128]{1,0:T(8,128)S(1)} %bitcast.292), channel_id=1, source_target_pairs={{0,24},{4,28},{8,0},{12,4},{16,8},{20,12},{24,16},{28,20},{1,25},{... | collective-permute-start | bytes 196616 | tf_op jit(solution)/shard_map/ppermute | solution.py:21
  58.5 32.0 %collective-permute-start.14 = (bf16[2,384,128]{2,1,0:T(8,128)(2,1)S(1)}, bf16[2,384,128]{2,1,0:T(8,128)(2,1)S(1)}, u32[]{:S(2)}, u32[]{:S(2)}) collective-permute-start(bf16[2,384,128]{2,1,0:T(8,128)(2,1)S(1)} %get-tuple-element.33), channel_id=1, source_target_pairs={{0,28},{4,0},{8,4},{12,8},{16,12},{20,16},{24,20},{28,24},{1,29},{... | collective-permute-start | bytes 589832 | tf_op jit(solution)/shard_map/ppermute | solution.py:21
  58.6 30.6 %collective-permute-start.15 = (bf16[2,384,128]{2,1,0:T(8,128)(2,1)S(1)}, bf16[2,384,128]{2,1,0:T(8,128)(2,1)S(1)}, u32[]{:S(2)}, u32[]{:S(2)}) collective-permute-start(bf16[2,384,128]{2,1,0:T(8,128)(2,1)S(1)} %get-tuple-element.32), channel_id=1, source_target_pairs={{0,24},{4,28},{8,0},{12,4},{16,8},{20,12},{24,16},{28,20},{1,25},{... | collective-permute-start | bytes 589832 | tf_op jit(solution)/shard_map/ppermute | solution.py:21
  59.3 29.7 %collective-permute-start.16 = (bf16[2,384,128]{2,1,0:T(8,128)(2,1)S(1)}, bf16[2,384,128]{2,1,0:T(8,128)(2,1)S(1)}, u32[]{:S(2)}, u32[]{:S(2)}) collective-permute-start(bf16[2,384,128]{2,1,0:T(8,128)(2,1)S(1)} %get-tuple-element.31), channel_id=1, source_target_pairs={{0,20},{4,24},{8,28},{12,0},{16,4},{20,8},{24,12},{28,16},{1,21},{... | collective-permute-start | bytes 589832 | tf_op jit(solution)/shard_map/ppermute | solution.py:21
  85.0 13.2 %collective-permute-start.9 = (bf16[2,384,128]{2,1,0:T(8,128)(2,1)S(1)}, bf16[2,384,128]{2,1,0:T(8,128)(2,1)S(1)}, u32[]{:S(2)}, u32[]{:S(2)}) collective-permute-start(bf16[2,384,128]{2,1,0:T(8,128)(2,1)S(1)} %get-tuple-element.30), channel_id=1, source_target_pairs={{0,28},{4,0},{8,4},{12,8},{16,12},{20,16},{24,20},{28,24},{1,29},{... | collective-permute-start | bytes 589832 | tf_op jit(solution)/shard_map/ppermute | solution.py:21
  88.7 8.2 %collective-permute-start.10 = (bf16[2,384,128]{2,1,0:T(8,128)(2,1)S(1)}, bf16[2,384,128]{2,1,0:T(8,128)(2,1)S(1)}, u32[]{:S(2)}, u32[]{:S(2)}) collective-permute-start(bf16[2,384,128]{2,1,0:T(8,128)(2,1)S(1)} %get-tuple-element.29), channel_id=1, source_target_pairs={{0,24},{4,28},{8,0},{12,4},{16,8},{20,12},{24,16},{28,20},{1,25},{... | collective-permute-start | bytes 589832 | tf_op jit(solution)/shard_map/ppermute | solution.py:21
  89.0 7.7 %collective-permute-start.11 = (bf16[2,384,128]{2,1,0:T(8,128)(2,1)S(1)}, bf16[2,384,128]{2,1,0:T(8,128)(2,1)S(1)}, u32[]{:S(2)}, u32[]{:S(2)}) collective-permute-start(bf16[2,384,128]{2,1,0:T(8,128)(2,1)S(1)} %get-tuple-element.28), channel_id=1, source_target_pairs={{0,20},{4,24},{8,28},{12,0},{16,4},{20,8},{24,12},{28,16},{1,21},{... | collective-permute-start | bytes 589832 | tf_op jit(solution)/shard_map/ppermute | solution.py:21
  90.5 8.9 %copy-start.8 = (bf16[384,2,128]{2,0,1:T(8,128)(2,1)S(1)}, bf16[384,2,128]{2,0,1:T(8,128)(2,1)}, u32[]{:S(2)}) copy-start(bf16[384,2,128]{2,0,1:T(8,128)(2,1)} %copy-done.7) | copy-start | bytes 589828
  91.7 11.9 %copy-start.12 = (bf16[2,384,128]{2,1,0:T(8,128)(2,1)S(1)}, bf16[2,384,128]{2,1,0:T(8,128)(2,1)}, u32[]{:S(2)}) copy-start(bf16[2,384,128]{2,1,0:T(8,128)(2,1)} %fusion.1) | copy-start | bytes 589828
  100.0 6.4 %collective-permute-start.18 = (bf16[128,128]{1,0:T(8,128)(2,1)S(1)}, bf16[128,128]{1,0:T(8,128)(2,1)S(1)}, u32[]{:S(2)}, u32[]{:S(2)}) collective-permute-start(bf16[128,128]{1,0:T(8,128)(2,1)S(1)} %fusion.11), channel_id=1, source_target_pairs={{0,8},{4,12},{8,16},{12,20},{16,24},{20,28},{24,0},{28,4},{1,9},{5... | collective-permute-start | bytes 98312 | tf_op jit(solution)/shard_map/ppermute | solution.py:21
  104.1 4.3 %collective-permute-start.17 = (bf16[128,128]{1,0:T(8,128)(2,1)S(1)}, bf16[128,128]{1,0:T(8,128)(2,1)S(1)}, u32[]{:S(2)}, u32[]{:S(2)}) collective-permute-start(bf16[128,128]{1,0:T(8,128)(2,1)S(1)} %fusion.10), channel_id=1, source_target_pairs={{0,4},{4,8},{8,12},{12,16},{16,20},{20,24},{24,28},{28,0},{1,5},{5... | collective-permute-start | bytes 98312 | tf_op jit(solution)/shard_map/ppermute | solution.py:21
  (11 other events, 21.8 us)
